TPU v7x, 32 devices: a whole 2x2x4 slice. The times are simulated.
32 devices in a mesh: dp: 4 (over y, core), fsdp: 8 (over z, x).
Axes of the slice: x: 2, y: 2, z: 4, core: 2. Of those that a mesh axis runs over, the one named last changes fastest.
Arguments:
- inputs: bfloat16 [32768, 512], P(('dp', 'fsdp')), may hold values from -6 to 6
- seq_lengths: int32 [32, 8], P(('dp', 'fsdp')), may hold values from 1 to 256, 1024 in all within a row
- query_weight: bfloat16 [512, 512], P(('dp', 'fsdp')), may hold values from -0.25 to 0.25
- key_weight: bfloat16 [512, 512], P(('dp', 'fsdp')), may hold values from -0.25 to 0.25
- value_weight: bfloat16 [512, 512], P(('dp', 'fsdp')), may hold values from -0.25 to 0.25
- output_weight: bfloat16 [512, 512], P(('dp', 'fsdp')), may hold values from -2 to 2
- query_bias: bfloat16 [512], P(('dp', 'fsdp')), may hold values from -3 to 3
- value_bias: bfloat16 [512], P(('dp', 'fsdp')), may hold values from -3 to 3
- output_bias: bfloat16 [512], P(('dp', 'fsdp')), may hold values from -3 to 3
- first_gain: bfloat16 [512], P(('dp', 'fsdp')), may hold values from 0.25 to 1.75
- first_shift: bfloat16 [512], P(('dp', 'fsdp')), may hold values from -3 to 3
- inner_weight: bfloat16 [512, 2048], P(('dp', 'fsdp')), may hold values from -0.25 to 0.25
- inner_bias: bfloat16 [2048], P(('dp', 'fsdp')), may hold values from -3 to 3
- outer_weight: bfloat16 [2048, 512], P(('dp', 'fsdp')), may hold values from -0.125 to 0.125
- outer_bias: bfloat16 [512], P(('dp', 'fsdp')), may hold values from -3 to 3
- final_gain: bfloat16 [512], P(('dp', 'fsdp')), may hold values from 0.25 to 1.75
- final_shift: bfloat16 [512], P(('dp', 'fsdp')), may hold values from -3 to 3
- cotangent: bfloat16 [32768, 512], P(('dp', 'fsdp')), may hold values from -6 to 6
Outputs:
- layer_out: bfloat16 [32768, 512], P(('dp', 'fsdp'))
- input_grad: float32 [32768, 512], P(('dp', 'fsdp'))
- query_weight_grad: float32 [512, 512], P(('dp', 'fsdp'))
- key_weight_grad: float32 [512, 512], P(('dp', 'fsdp'))
- value_weight_grad: float32 [512, 512], P(('dp', 'fsdp'))
- output_weight_grad: float32 [512, 512], P(('dp', 'fsdp'))
- query_bias_grad: float32 [512], P(('dp', 'fsdp'))
- value_bias_grad: float32 [512], P(('dp', 'fsdp'))
- output_bias_grad: float32 [512], P(('dp', 'fsdp'))
- first_gain_grad: float32 [512], P(('dp', 'fsdp'))
- first_shift_grad: float32 [512], P(('dp', 'fsdp'))
- inner_weight_grad: float32 [512, 2048], P(('dp', 'fsdp'))
- inner_bias_grad: float32 [2048], P(('dp', 'fsdp'))
- outer_weight_grad: float32 [2048, 512], P(('dp', 'fsdp'))
- outer_bias_grad: float32 [512], P(('dp', 'fsdp'))
- final_gain_grad: float32 [512], P(('dp', 'fsdp'))
- final_shift_grad: float32 [512], P(('dp', 'fsdp'))
Inputs may be any that keep to these rules, and one draw needn't show every extreme that they name: `seq_lengths`: each device's row of 8 lengths sums to 1024, and its longest is exactly 256.
All inputs are finite; a program needn't handle non-finite values.
Results may differ from a plain program's by a relative error of at most 0.013.
The roundings to bfloat16 on the way count: a program that leaves them out, or rounds other values in their place, can miss the bound.
Values may be sent and summed in bfloat16 or wider, within the bound.
A program may use at most 192 MiB of HBM per device.

v0:
```python
from functools import partial
import math
import types

import jax
import jax.numpy as jnp
from jax import lax
from jax.experimental import pallas as pl
from jax.experimental.pallas import tpu as pltpu
from jax.sharding import PartitionSpec as P

norm_eps = 1e-05
Q_BIAS, V_BIAS, O_BIAS, GAIN_ONE, SHIFT_ONE, U_BIAS, GAIN_TWO, SHIFT_TWO = range(8)
BLOCK = 256
STARTS, PACKED = (0, 640, 1152), 512
PAIRS = ((0, 256), (256, 384), (384, 512))
LANES = 128
far = -1e30


def nn(left, right):
    return jnp.dot(left, right, preferred_element_type=jnp.float32)


def tn(left, right):
    return lax.dot_general(left, right, (((0,), (0,)), ((), ())), preferred_element_type=jnp.float32)


def nt(left, right):
    return lax.dot_general(left, right, (((1,), (1,)), ((), ())), preferred_element_type=jnp.float32)


def low(values):
    return values.astype(jnp.bfloat16)


def wide(values):
    return values.astype(jnp.float32)


def iota(shape, axis):
    return lax.broadcasted_iota(jnp.int32, shape, axis)


def matrix(ref):
    return ref[...].reshape(-1, ref.shape[-1])


def block_of(i):
    return pl.ds(BLOCK * i if isinstance(i, int) else pl.multiple_of(i * BLOCK, BLOCK), BLOCK)


def lanes_of(first):
    return pl.ds(first if isinstance(first, int) else pl.multiple_of(first, LANES), LANES)


def boundaries(lengths):
    starts, ends, at = [], [], 0
    for s in range(lengths.shape[1]):
        starts.append(at)
        at = at + lengths[0, s]
        ends.append(at)
    before, after = [], []
    for edge in (BLOCK, 2 * BLOCK, 3 * BLOCK):
        tail, head = 0, 0
        for start, end in zip(starts, ends):
            across = (start < edge) & (end > edge)
            tail = tail + jnp.where(across, edge - start, 0)
            head = head + jnp.where(across, end - edge, 0)
        before.append(tail)
        after.append(head)
    return starts, ends, before, after


class Attention:
    def __init__(self, lengths):
        self.starts, self.ends, self.before, self.after = boundaries(lengths)
        self.rows = iota((BLOCK, LANES), 0)
        self.lanes = iota((BLOCK, LANES), 1)
        self.left = self.lanes < 64

    def members(self, block):
        rows, lanes = self.rows + block * BLOCK, lax.rem(self.lanes, 64)
        marks = jnp.zeros((BLOCK, LANES), jnp.float32)
        for s, (start, end) in enumerate(zip(self.starts, self.ends)):
            inside = (rows >= start) & (rows < end) & (lanes == s)
            marks = jnp.where(inside, 1.0, marks)
        return marks

    def merged(self, blocks):
        return [*blocks, *[jnp.where(self.in_head(i), blocks[i + 1], blocks[i]) for i in range(3)]]

    def half(self, side):
        return self.left if side == 0 else ~self.left

    def in_head(self, edge):
        return self.rows < self.after[edge]

    def in_tail(self, edge):
        return self.rows >= BLOCK - self.before[edge]

    def pick(self, parts):
        out = []
        for i in range(4):
            block = parts[i]
            if i < 3:
                block = jnp.where(self.in_tail(i), parts[4 + i], block)
            if i > 0:
                block = jnp.where(self.in_head(i - 1), parts[3 + i], block)
            out.append(block)
        return out

    def gather_sums(self, parts):
        out = []
        for i in range(4):
            block = parts[i]
            if i < 3:
                block = block + jnp.where(self.in_head(i), 0.0, parts[4 + i])
            if i > 0:
                block = block + jnp.where(self.in_head(i - 1), parts[3 + i], 0.0)
            out.append(block)
        return out

    def units(self, blocks):
        out = []
        for i in range(4):
            block = blocks[i]
            if i < 3:
                block = jnp.where(self.in_tail(i), 0.0, block)
            if i > 0:
                block = jnp.where(self.in_head(i - 1), 0.0, block)
            out.append(block)
        for i in range(3):
            tail = jnp.where(self.in_tail(i), blocks[i], 0.0)
            out.append(jnp.where(self.in_head(i), blocks[i + 1], tail))
        return out


def square_of(r, part):
    first = STARTS[part]
    return r.wqkv[:, :, :, :, :, first : first + 512].reshape(512, 512)


def mark(r, at):
    for unit, marks in enumerate(at.merged([at.members(i) for i in range(4)])):
        r.marks[unit] = low(marks)


def project(r, at, part):
    dest = (r.q, r.k, r.v)[part]

    def put(unit, product):
        marks = wide(r.marks[unit])
        beside = (marks, jnp.where(lax.rem(at.lanes, 64) < 8, far - far * marks, 0.0), 1.0)[part]
        for pair in range(4):
            both = product[:, LANES * pair : LANES * (pair + 1)]
            for side in range(2):
                dest[2 * pair + side, unit] = low(jnp.where(at.half(side), both, beside))

    head = [iota((BLOCK, 512), 0) < count for count in at.after]
    for i in range(4):
        product = nn(r.x[block_of(i)], square_of(r, part))
        if part == 0:
            product = (product + r.vec[Q_BIAS : Q_BIAS + 1]) * 0.125
        elif part == 2:
            product = product + r.vec[V_BIAS : V_BIAS + 1]
        put(i, product)
        if i > 0:
            put(3 + i, jnp.where(head[i - 1], product, before))
        before = product


def attend(r, at, pair):
    outs = []
    for side in range(2):
        head = 2 * pair + side
        parts = []
        for unit in range(7):
            scores = nt(r.k[head, unit], r.q[head, unit])
            top = jnp.max(scores, axis=0, keepdims=True)
            grown = low(jnp.exp(scores - top))
            r.e[head, unit] = grown
            parts.append(tn(grown, r.v[head, unit]))
        outs.append(at.pick(parts))
    columns = lanes_of(pair * LANES)
    for i in range(4):
        even, odd = outs[0][i], outs[1][i]
        share = 1.0 / pltpu.roll(jnp.where(at.left, odd, even), 64, 1)
        mixed = jnp.where(at.left, even, odd) * share
        r.combined[BLOCK * i : BLOCK * (i + 1), columns] = low(mixed)
        r.share[BLOCK * i : BLOCK * (i + 1), columns] = share


def normal(values):
    center = values - jnp.mean(values, axis=-1, keepdims=True)
    spread = jnp.mean(center * center, axis=-1, keepdims=True)
    scale = lax.rsqrt(spread + norm_eps)
    return center * scale, scale


def normal_back(grad, normed, scale):
    return scale * (
        grad
        - jnp.mean(grad, axis=-1, keepdims=True)
        - normed * jnp.mean(grad * normed, axis=-1, keepdims=True)
    )


def sums(values):
    return jnp.sum(values, axis=0, keepdims=True)


def attended_rows(r, i):
    rows = block_of(i)
    attended = nn(r.combined[rows], matrix(r.wo)) + r.vec[O_BIAS : O_BIAS + 1]
    normed, scale = normal(wide(r.x[rows]) + attended)
    r.normed[rows] = normed
    r.scale[rows] = jnp.broadcast_to(scale, (BLOCK, LANES))
    r.hidden[rows] = low(normed * r.vec[GAIN_ONE : GAIN_ONE + 1] + r.vec[SHIFT_ONE : SHIFT_ONE + 1])


def active_rows(r, side, i):
    rows = block_of(i)
    hidden_low = r.hidden[rows]
    slope = math.sqrt(2 / math.pi)
    for part in (2 * side, 2 * side + 1):
        columns = slice(512 * part, 512 * (part + 1))
        inner = nn(hidden_low, r.wi[:, :, :, :, :, columns].reshape(512, 512)) + r.ib[:, columns]
        square = inner * inner
        half = 0.5 * jnp.tanh(inner * (slope + (slope * 0.044715) * square)) + 0.5
        active = inner * half
        r.active[rows, columns] = low(active)
        turn = half + active * (1.0 - half) * (2 * slope + (6 * slope * 0.044715) * square)
        r.turn[rows, columns] = low(turn)


def final_rows(r, i):
    rows = block_of(i)
    hidden = r.normed[rows] * r.vec[GAIN_ONE : GAIN_ONE + 1] + r.vec[SHIFT_ONE : SHIFT_ONE + 1]
    outer = nn(r.active[rows], matrix(r.wu)) + r.vec[U_BIAS : U_BIAS + 1]
    normed, scale = normal(outer + hidden + wide(r.x[rows]))
    gain = r.vec[GAIN_TWO : GAIN_TWO + 1]
    r.out[rows] = low(normed * gain + r.vec[SHIFT_TWO : SHIFT_TWO + 1])
    grad = wide(r.cot[rows])
    r.gvec[GAIN_TWO : GAIN_TWO + 1] += sums(grad * normed)
    r.gvec[SHIFT_TWO : SHIFT_TWO + 1] += sums(grad)
    grad_two = normal_back(grad * gain, normed, scale)
    r.grad[rows] = grad_two
    grad_outer = low(grad_two)
    r.grad_outer[rows] = grad_outer
    r.gvec[U_BIAS : U_BIAS + 1] += sums(wide(grad_outer))


def rows_of(ref, quarter):
    return ref[quarter // 2, quarter % 2].reshape(-1, ref.shape[-1])


def outer_weight_grad(r, side):
    for quarter in range(4):
        rows, columns = slice(512 * quarter, 512 * (quarter + 1)), slice(256 * side, 256 * (side + 1))
        product = low(tn(r.active[:, rows], r.grad_outer[:, columns]))
        r.gu[quarter // 2, quarter % 2, :, :, :, columns] = product.reshape(4, 2, -1, 256)


def inner_rows(r, i):
    rows = block_of(i)
    grad_outer = r.grad_outer[rows]
    for part in range(4):
        columns = slice(512 * part, 512 * (part + 1))
        grad_inner = low(nt(grad_outer, rows_of(r.wu, part)) * wide(r.turn[rows, columns]))
        r.active[rows, columns] = grad_inner
        r.gib[:, columns] += sums(wide(grad_inner))


def inner_weight_grad(r, side):
    for half in range(2):
        for part in (2 * side, 2 * side + 1):
            columns = slice(512 * part, 512 * (part + 1))
            product = low(tn(r.hidden[:, 256 * half : 256 * (half + 1)], r.active[:, columns]))
            r.gi[half, :, :, :, :, columns] = product.reshape(2, 4, 2, -1, 512)


def hidden_rows(r, i):
    rows = block_of(i)
    grad_two = r.grad[rows]
    grad_hidden = nt(r.active[rows], matrix(r.wi)) + grad_two
    normed = r.normed[rows]
    r.gvec[GAIN_ONE : GAIN_ONE + 1] += sums(grad_hidden * normed)
    r.gvec[SHIFT_ONE : SHIFT_ONE + 1] += sums(grad_hidden)
    gain = r.vec[GAIN_ONE : GAIN_ONE + 1]
    grad_one = normal_back(grad_hidden * gain, normed, r.scale[rows, 0:1])
    r.grad[rows] = grad_two + grad_one
    attended = low(grad_one)
    r.attended[rows] = attended
    r.gvec[O_BIAS : O_BIAS + 1] += sums(wide(attended))
    r.grad_outer[rows] = low(nt(attended, matrix(r.wo)))


def output_weight_grad(r):
    for half in range(2):
        product = low(tn(r.combined[:, 256 * half : 256 * (half + 1)], r.attended[...]))
        r.go[half] = product.reshape(r.go.shape[1:])


def attend_back(r, at, pair):
    columns = lanes_of(pair * LANES)
    ones = low(jnp.where((iota((LANES, LANES), 0) < 64) == (iota((LANES, LANES), 1) < 64), 1.0, 0.0))
    sides = [[], []]
    for i in range(4):
        rows = slice(BLOCK * i, BLOCK * (i + 1))
        grad = wide(r.grad_outer[rows, columns])
        share = r.share[rows, columns]
        product = grad * wide(r.combined[rows, columns])
        high = low(product)
        total = nn(high, ones) + nn(low(product - wide(high)), ones)
        total = pltpu.roll(-(total * share), 64, 1)
        rest = total - wide(low(total))
        lanes = lax.rem(at.lanes, 64)
        beside = jnp.where(lanes == 0, total, jnp.where(lanes == 1, rest, 0.0))
        grad = grad * share
        for side in range(2):
            sides[side].append(jnp.where(at.half(side), grad, beside))
    found = [[], [], []]
    for side in range(2):
        head = 2 * pair + side
        parts = [[], [], []]
        for unit, grad in enumerate(at.units(sides[side])):
            grad = low(grad)
            grown = r.e[head, unit]
            scores = low(wide(grown) * nt(r.v[head, unit], grad))
            parts[0].append(tn(scores, r.k[head, unit]))
            parts[1].append(nn(scores, r.q[head, unit]))
            parts[2].append(nn(grown, grad))
        for which in range(3):
            found[which].append(at.gather_sums(parts[which]))
    for which in range(3):
        total = 0.0
        for i in range(4):
            both = jnp.where(at.left, found[which][0][i], found[which][1][i])
            both = low(both * 0.125 if which == 0 else both)
            (r.dq, r.dk, r.dv)[which][BLOCK * i : BLOCK * (i + 1), columns] = both
            total = total + wide(both)
        if which != 1:
            r.gvec[which // 2 : which // 2 + 1, columns] = sums(total)


def qkv_weight_grad(r, piece):
    first, last = PAIRS[piece]
    for part, grads in enumerate((r.dq, r.dk, r.dv)):
        start = 3 * first + (last - first) * part
        for half in range(2):
            product = low(tn(r.x[:, 256 * half : 256 * (half + 1)], grads[:, first:last]))
            columns = slice(start, start + last - first)
            r.gqkv[half, :, :, :, :, columns] = product.reshape(2, 4, 2, -1, last - first)


def input_rows(r, i):
    rows = block_of(i)
    total = r.grad[rows]
    for part, grads in enumerate((r.dq, r.dk, r.dv)):
        total = total + nt(grads[rows], square_of(r, part))
    r.grad[rows] = total


(
    ZERO, MARK, UNPACK, PROJECT_Q, PROJECT_K, PROJECT_V, ATTEND, ATTENDED, ACTIVE0, ACTIVE1, FINAL, OUTER_GRAD0, OUTER_GRAD1, INNER,
    INNER_GRAD0, INNER_GRAD1, HIDDEN, OUTPUT_GRAD, PACK_EARLY, BACK, QKV_GRAD0, QKV_GRAD1, QKV_GRAD2, PACK_LATE, INPUT,
) = range(25)
LOCAL = [step for step in range(25) if step not in (UNPACK, PACK_EARLY, PACK_LATE)]


def all_rows(rows, r, *given):
    for i in range(4):
        rows(r, *given, i)


def rows_by_two(rows, r):
    def two(i, carried):
        rows(r, 2 * i)
        rows(r, 2 * i + 1)
        return carried

    lax.fori_loop(0, 2, two, 0)


def zero(r):
    r.gvec[...] = jnp.zeros_like(r.gvec)
    r.gib[...] = jnp.zeros_like(r.gib)


def steps_of(r):
    at = Attention(r.lengths)
    steps = {
        ZERO: partial(zero, r),
        MARK: partial(mark, r, at),
        UNPACK: partial(unpack_vectors, r),
        ATTEND: partial(attend, r, at),
        ATTENDED: partial(all_rows, attended_rows, r),
        FINAL: partial(all_rows, final_rows, r),
        INNER: partial(all_rows, inner_rows, r),
        HIDDEN: partial(rows_by_two, hidden_rows, r),
        OUTPUT_GRAD: partial(output_weight_grad, r),
        PACK_EARLY: partial(pack_sums, r, True),
        BACK: partial(attend_back, r, at),
        PACK_LATE: partial(pack_sums, r, False),
        INPUT: partial(rows_by_two, input_rows, r),
    }
    for i in range(3):
        steps[PROJECT_Q + i] = partial(project, r, at, i)
        steps[QKV_GRAD0 + i] = partial(qkv_weight_grad, r, i)
    for i in range(2):
        steps[ACTIVE0 + i] = partial(all_rows, active_rows, r, i)
        steps[OUTER_GRAD0 + i] = partial(outer_weight_grad, r, i)
        steps[INNER_GRAD0 + i] = partial(inner_weight_grad, r, i)
    return steps


def always():
    return lax.axis_index("dp") >= 0


def take(step):
    pl.when(always())(step)


def over_pairs(step, between):
    def body(pair, carried):
        for n in range(4):
            pl.when(pair == n)(partial(between, n))
        step(pair)
        return carried

    lax.fori_loop(0, 4, body, 0)


def run_local(r):
    steps = steps_of(r)
    for step in LOCAL:
        if step in (ATTEND, BACK):
            over_pairs(steps[step], lambda n: None)
        else:
            take(steps[step])
MESH_ID = pl.DeviceIdType.MESH


def place():
    outer, inner = lax.axis_index("dp"), lax.axis_index("fsdp")
    return outer // 2, outer % 2, inner // 2, inner % 2


def device_at(y, core, z, x):
    return (y * 2 + core, z * 2 + x)


def greet_partners():
    y, core, z, x = place()
    partners = [
        device_at(y, 1 - core, z, x),
        device_at(1 - y, core, z, x),
        device_at(y, core, z, 1 - x),
        device_at(1 - y, core, z, 1 - x),
    ] + [device_at(y, core, (z + step) % 4, x) for step in (1, 2, 3)]
    barrier = pltpu.get_barrier_semaphore()
    for partner in partners:
        pl.semaphore_signal(barrier, inc=1, device_id=partner, device_id_type=MESH_ID)
    return lambda: pl.semaphore_wait(barrier, len(partners))


def remote(source, target, send_sem, recv_sem, to):
    return pltpu.make_async_remote_copy(
        src_ref=source,
        dst_ref=target,
        send_sem=send_sem,
        recv_sem=recv_sem,
        device_id=to,
        device_id_type=MESH_ID,
    )


class Corner:
    def __init__(self):
        y, core, z, x = place()
        self.y, self.core, self.z, self.x = y, core, z, x
        self.ya, self.xa = jnp.where(core == 0, y, 1 - y), jnp.where(core == 0, 1 - x, x)
        self.yb, self.xb = jnp.where(core == 0, 1 - y, y), jnp.where(core == 0, x, 1 - x)
        self.partner_a = device_at(self.ya, core, z, self.xa)
        self.partner_b = device_at(self.yb, core, z, self.xb)
        self.sibling = device_at(y, 1 - core, z, x)
        self.across = device_at(1 - y, core, z, 1 - x)

    def along_z(self, step):
        return device_at(self.y, self.core, (self.z + step) % 4, self.x)


class Gather:
    def __init__(self, corner, own, whole, send_sem, recv_sem):
        self.at, self.own, self.whole = corner, own, whole
        self.send_sem, self.recv_sem = send_sem, recv_sem

    def to_z(self, step):
        at = self.at
        slot = self.whole.at[at.y, at.core, at.z, at.x]
        return remote(
            self.own, slot, self.send_sem.at[step - 1], self.recv_sem.at[step - 1], at.along_z(step)
        )

    def line(self, y, x, number, to):
        line = self.whole.at[y, self.at.core, :, x]
        return remote(line, line, self.send_sem.at[number], self.recv_sem.at[number], to)

    def to_a(self):
        return self.line(self.at.y, self.at.x, 3, self.at.partner_a)

    def to_b(self, part):
        at = self.at
        y, x = ((at.y, at.x), (at.ya, at.xa))[part]
        return self.line(y, x, 4 + part, at.partner_b)

    def to_sibling(self, part):
        at = self.at
        y, x = ((at.y, at.x), (at.ya, at.xa), (at.yb, at.xb), (1 - at.y, 1 - at.x))[part]
        return self.line(y, x, 6 + part, at.sibling)

    def phase(self, number):
        if number == 0:
            for step in (2, 1, 3):
                self.to_z(step).start()
            at = self.at
            self.whole[at.y, at.core, at.z, at.x] = self.own[...]
        elif number == 1:
            for step in (1, 2, 3):
                self.to_z(step).wait_recv()
            self.to_a().start()
            self.to_b(0).start()
            self.to_sibling(0).start()
        elif number == 2:
            self.to_a().wait_recv()
            self.to_b(1).start()
            self.to_sibling(1).start()
        elif number == 3:
            self.to_b(0).wait_recv()
            self.to_sibling(2).start()
            self.to_b(1).wait_recv()
            self.to_sibling(3).start()
        elif number == 4:
            for part in range(4):
                self.to_sibling(part).wait_recv()

    def finish(self):
        for step in (1, 2, 3):
            self.to_z(step).wait_send()
        self.to_a().wait_send()
        for part in range(2):
            self.to_b(part).wait_send()
        for part in range(4):
            self.to_sibling(part).wait_send()


class GatherPlaneFirst(Gather):
    def slot(self, y, x, number, to):
        slot = self.whole.at[y, self.at.core, self.at.z, x]
        return remote(slot, slot, self.send_sem.at[number], self.recv_sem.at[number], to)

    def to_a(self):
        return self.slot(self.at.y, self.at.x, 3, self.at.partner_a)

    def to_b(self, part):
        at = self.at
        y, x = ((at.y, at.x), (at.ya, at.xa))[part]
        return self.slot(y, x, 4 + part, at.partner_b)

    def plane(self, z, number, to):
        plane = self.whole.at[:, self.at.core, z]
        return remote(plane, plane, self.send_sem.at[number], self.recv_sem.at[number], to)

    def to_z(self, step):
        return self.plane(self.at.z, step - 1, self.at.along_z(step))

    def to_sibling(self, part):
        return self.plane((self.at.z + part) % 4, 6 + part, self.at.sibling)

    def phase(self, number):
        at = self.at
        if number == 0:
            self.whole[at.y, at.core, at.z, at.x] = self.own[...]
            self.to_a().start()
            self.to_b(0).start()
        elif number == 1:
            self.to_a().wait_recv()
            self.to_b(1).start()
        elif number == 2:
            self.to_b(0).wait_recv()
            self.to_b(1).wait_recv()
            for step in (2, 1, 3):
                self.to_z(step).start()
            self.to_sibling(0).start()
        elif number == 3:
            for step in (1, 3, 2):
                self.to_z(step).wait_recv()
                self.to_sibling(4 - step).start()
        elif number == 4:
            for part in range(4):
                self.to_sibling(part).wait_recv()


class Scatter:
    def __init__(self, corner, whole, out, got_core, got_b, got_a, got_z, send_sem, recv_sem):
        self.at, self.whole, self.out = corner, whole, out
        self.got_core, self.got_b, self.got_a, self.got_z = got_core, got_b, got_a, got_z
        self.send_sem, self.recv_sem = send_sem, recv_sem

    def sems(self, number):
        return self.send_sem.at[number], self.recv_sem.at[number]

    def to_sibling(self):
        return remote(
            self.whole.at[:, 1 - self.at.core], self.got_core, *self.sems(0), self.at.sibling
        )

    def to_b(self, part):
        at = self.at
        y, x = ((at.yb, at.xb), (1 - at.y, 1 - at.x))[part]
        return remote(
            self.whole.at[y, at.core, :, x], self.got_b.at[part], *self.sems(1 + part), at.partner_b
        )

    def to_a(self):
        at = self.at
        return remote(
            self.whole.at[at.ya, at.core, :, at.xa], self.got_a, *self.sems(3), at.partner_a
        )

    def to_z(self, step):
        at = self.at
        return remote(
            self.whole.at[at.y, at.core, (at.z + step) % 4, at.x],
            self.got_z.at[step - 1],
            *self.sems(3 + step),
            at.along_z(step),
        )

    def add_line(self, y, x, other):
        core = self.at.core
        for z in range(4):
            total = self.whole[y, core, z, x].astype(jnp.float32) + other(z).astype(jnp.float32)
            self.whole[y, core, z, x] = total.astype(self.whole.dtype)

    def add_core(self, y, x):
        self.add_line(y, x, lambda z: self.got_core[y, z, x])

    def phase(self, number):
        at = self.at
        if number == 0:
            self.to_sibling().start()
        elif number == 1:
            self.to_sibling().wait_recv()
            self.add_core(at.yb, at.xb)
            self.to_b(0).start()
            self.add_core(1 - at.y, 1 - at.x)
            self.to_b(1).start()
            self.add_core(at.ya, at.xa)
            self.add_core(at.y, at.x)
        elif number == 2:
            self.to_b(1).wait_recv()
            self.add_line(at.ya, at.xa, lambda z: self.got_b[1, z])
            self.to_a().start()
            self.to_b(0).wait_recv()
            self.add_line(at.y, at.x, lambda z: self.got_b[0, z])
        elif number == 3:
            self.to_a().wait_recv()
            self.add_line(at.y, at.x, lambda z: self.got_a[z])
            for step in (2, 1, 3):
                self.to_z(step).start()
        elif number == 4:
            total = self.whole[at.y, at.core, at.z, at.x].astype(jnp.float32)
            for step in (1, 2, 3):
                self.to_z(step).wait_recv()
                total = total + self.got_z[step - 1].astype(jnp.float32)
            self.out[...] = total

    def finish(self):
        self.to_sibling().wait_send()
        for part in range(2):
            self.to_b(part).wait_send()
        self.to_a().wait_send()
        for step in (1, 2, 3):
            self.to_z(step).wait_send()


class ScatterDirect(Scatter):
    def phase(self, number):
        at = self.at
        if number == 1:
            self.to_sibling().wait_recv()
            self.add_core(1 - at.y, 1 - at.x)
            self.to_b(1).start()
            self.add_core(at.yb, at.xb)
            self.to_b(0).start()
            self.add_core(at.ya, at.xa)
            self.to_a().start()
            self.add_core(at.y, at.x)
        elif number == 2:
            self.to_a().wait_recv()
            for part in range(2):
                self.to_b(part).wait_recv()
            for z in range(4):
                line = self.whole[at.y, at.core, z, at.x].astype(jnp.float32)
                for got in (self.got_a[z], self.got_b[0, z], self.got_b[1, z]):
                    line = line + got.astype(jnp.float32)
                self.whole[at.y, at.core, z, at.x] = line.astype(self.whole.dtype)
            for step in (2, 1, 3):
                self.to_z(step).start()
        elif number != 3:
            super().phase(number)

    def to_b(self, part):
        at = self.at
        y, x, to = ((at.yb, at.xb, at.partner_b), (1 - at.y, 1 - at.x, at.across))[part]
        return remote(self.whole.at[y, at.core, :, x], self.got_b.at[part], *self.sems(1 + part), to)


class ScatterPlaneLast(Scatter):
    def to_z(self, step):
        at = self.at
        return remote(
            self.whole.at[:, at.core, (at.z + step) % 4],
            self.got_z.at[step - 1],
            *self.sems(3 + step),
            at.along_z(step),
        )

    def to_b(self, part):
        at = self.at
        y, x = ((at.yb, at.xb), (1 - at.y, 1 - at.x))[part]
        source = self.whole.at[y, at.core, at.z, x]
        return remote(source, self.got_b.at[part], *self.sems(1 + part), at.partner_b)

    def to_a(self):
        at = self.at
        source = self.whole.at[at.ya, at.core, at.z, at.xa]
        return remote(source, self.got_a, *self.sems(3), at.partner_a)

    def add(self, y, z, x, *others):
        core = self.at.core
        total = self.whole[y, core, z, x].astype(jnp.float32)
        for other in others:
            total = total + other.astype(jnp.float32)
        self.whole[y, core, z, x] = total.astype(self.whole.dtype)

    def phase(self, number):
        at = self.at
        places = [(y, x) for y in range(2) for x in range(2)]
        if number == 0:
            self.to_sibling().start()
        elif number == 1:
            self.to_sibling().wait_recv()
            for step in (2, 1, 3, 0):
                z = (at.z + step) % 4
                for y, x in places:
                    self.add(y, z, x, self.got_core[y, z, x])
                if step:
                    self.to_z(step).start()
        elif number == 2:
            for step in (1, 2, 3):
                self.to_z(step).wait_recv()
            for y, x in places:
                self.add(y, at.z, x, *[self.got_z[step, y, x] for step in range(3)])
            for part in range(2):
                self.to_b(part).start()
        elif number == 3:
            self.to_b(1).wait_recv()
            self.add(at.ya, at.z, at.xa, self.got_b[1])
            self.to_a().start()
            self.to_b(0).wait_recv()
        elif number == 4:
            self.to_a().wait_recv()
            total = self.whole[at.y, at.core, at.z, at.x].astype(jnp.float32)
            self.out[...] = total + self.got_b[0].astype(jnp.float32) + self.got_a[...].astype(jnp.float32)
LEAD = (2, 2, 4, 2)
TOKENS, WIDTH = 1024, 512
BF, F32 = jnp.bfloat16, jnp.float32
AXES = ("dp", "fsdp")
SHARDS = dict(wqkv=(16, 1664), wo=(16, 512), wi=(16, 2048), wu=(64, 512))


def local_scratch():
    units, tokens = (8, 7, BLOCK, LANES), (TOKENS, WIDTH)
    return dict(
        q=(units, BF),
        k=(units, BF),
        v=(units, BF),
        e=((8, 7, BLOCK, BLOCK), BF),
        marks=((7, BLOCK, LANES), BF),
        share=(tokens, F32),
        combined=(tokens, BF),
        normed=(tokens, F32),
        scale=((TOKENS, LANES), F32),
        hidden=(tokens, BF),
        active=((TOKENS, 2048), BF),
        turn=((TOKENS, 2048), BF),
        grad_outer=(tokens, BF),
        attended=(tokens, BF),
    )


def call(kernel, inputs, spaces, outputs, scratch, sems, **params):
    names = [*inputs, *outputs, *scratch, *sems]

    def body(*refs):
        kernel(types.SimpleNamespace(**dict(zip(names, refs, strict=True))))

    made = pl.pallas_call(
        body,
        out_shape=[jax.ShapeDtypeStruct(*given) for given in outputs.values()],
        in_specs=[pl.BlockSpec(memory_space=spaces.get(name, pltpu.VMEM)) for name in inputs],
        out_specs=[pl.BlockSpec(memory_space=spaces.get(name, pltpu.VMEM)) for name in outputs],
        scratch_shapes=[pltpu.VMEM(*given) for given in scratch.values()]
        + [pltpu.SemaphoreType.DMA(shape) for shape in sems.values()],
        compiler_params=pltpu.CompilerParams(vmem_limit_bytes=63 << 20, **params),
    )(*inputs.values())
    return types.SimpleNamespace(**dict(zip(outputs, made, strict=True)))


def chosen_lanes(count):
    shape = (LANES, 32 * count)
    return low(jnp.where(iota(shape, 0) == lax.rem(iota(shape, 1), count), 1.0, 0.0))


def of_owner(rows, count):
    shape = (rows, 32 * count)
    return lax.rem(iota(shape, 0), 32) == lax.div(iota(shape, 1), count)


def chosen_rows():
    row, column = iota((288, 512), 0), iota((288, 512), 1)
    return low(jnp.where(column == lax.rem(row, 32) * 16 + lax.div(row, 32), 1.0, 0.0))


def unpack_vectors(r):
    packed = r.wqkv[:, :, :, :, :, PACKED : PACKED + LANES].reshape(512, LANES)
    packed = low(nn(chosen_rows(), packed))
    vectors = jnp.where(of_owner(256, 16), nn(packed[:256], chosen_lanes(16)), 0.0)
    for kind in range(8):
        r.vec[kind : kind + 1] = sums(vectors[32 * kind : 32 * (kind + 1)])
    r.ib[...] = sums(jnp.where(of_owner(32, 64), nn(packed[256:], chosen_lanes(64)), 0.0))


def pack_sums(r, early):
    def placed(values, count):
        alone = jnp.where(of_owner(32, count), values, 0.0)
        high = low(alone)
        lanes = chosen_lanes(count)
        return nt(high, lanes) + nt(low(alone - wide(high)), lanes)

    rows = [placed(r.gvec[kind : kind + 1], 16) for kind in (range(2, 8) if early else range(2))]
    rows += [placed(r.gib[...], 64)] if early else []
    chosen = chosen_rows()[64:] if early else chosen_rows()[:64]
    packed = low(tn(chosen, low(jnp.concatenate(rows, axis=0)))).reshape(*LEAD, 16, LANES)
    if not early:
        packed = packed + r.gqkv[:, :, :, :, :, 1536:1664]
    r.gqkv[:, :, :, :, :, 1536:1664] = packed


Q, K, V, O, I0, I1, U0, U1 = range(8)
SU0, SU1, SI0, SI1, SO, SA, SB, SC = range(8, 16)
X_HERE, COT_HERE, OUT_AWAY, GRAD_AWAY0, GRAD_AWAY1 = range(100, 105)
PLAN = [
    (K, 0), (U1, 0), (Q, 0), (V, 0), ZERO, MARK, X_HERE, (U1, 1), (O, 0), (I0, 0), (K, 1), (I1, 0), (Q, 1), (U0, 0),
    (K, 2), (V, 1), (Q, 2), (O, 1), (V, 2), (I0, 1), (Q, 3), (K, 3), (O, 2), (Q, 4), (U1, 2), UNPACK, PROJECT_Q,
    (K, 4), (V, 3), (I1, 1), PROJECT_K, (I0, 2), (V, 4), PROJECT_V,
    [ATTEND, [], [(U0, 1)], [(I1, 2), (O, 3)], [(I0, 3)]], (O, 4), (U0, 2), (I0, 4), ATTENDED, ACTIVE0, (I1, 3),
    (U1, 3), (U0, 3), (I1, 4), ACTIVE1, (U0, 4), (U1, 4), COT_HERE, FINAL, OUT_AWAY, OUTER_GRAD0, OUTER_GRAD1,
    (SU0, 0), INNER, (SU1, 0), INNER_GRAD0, (SI0, 0), INNER_GRAD1, (SI1, 0), (SU0, 1), HIDDEN, (SI0, 1), OUTPUT_GRAD,
    (SO, 0), PACK_EARLY, (SU1, 1), (SI1, 1),
    [BACK, [], [(SO, 1), (SI0, 2)], [QKV_GRAD0, (SA, 0), (SO, 2), (SU0, 2), (SI1, 2)], [QKV_GRAD1, (SB, 0), (SO, 3), (SA, 1), (SI0, 3), (SU0, 3), (SB, 1)]],
    (SU1, 2), QKV_GRAD2, (SA, 2), PACK_LATE, (SC, 0), (SI1, 3), (SB, 2), (SC, 1), INPUT, GRAD_AWAY0, GRAD_AWAY1,
    (SO, 4), (SB, 3), (SA, 3), (SU1, 3), (SC, 2), (SB, 4), (SU0, 4), (SC, 3), (SI0, 4), (SC, 4), (SI1, 4), (SA, 4),
    (SU1, 4),
]


def halves_of(buffer):
    first, second = [buffer.at[i : i + 512].reshape(*LEAD, 16, 2048) for i in (0, 512)]
    return first, second.at[:, :, :, :, :, 0:1664]


def direct_kernel(r):
    r.gi, r.gqkv = halves_of(r.turn)
    r.dq = r.wu.at[0].reshape(TOKENS, 512)
    r.dk = r.wu.at[1].reshape(TOKENS, 512)
    r.dv = r.attended
    r.cot = r.attended
    spare = [
        r.active.at[first : first + 16 * math.prod(lead)].reshape(*lead, 16, 2048)
        for lead, first in (((2, 4, 2), 0), ((2, 4), 256), ((4,), 384), ((3,), 448))
    ]
    local = [
        pltpu.make_async_copy(source, target, r.local.at[i])
        for i, (source, target) in enumerate(
            [(r.x_far, r.x), (r.cot_far, r.cot), (r.out, r.out_far)]
            + [(r.grad.at[BLOCK * i : BLOCK * (i + 1)], r.grad_far.at[BLOCK * i : BLOCK * (i + 1)]) for i in range(4)]
        )
    ]
    local[0].start()
    local[1].start()
    corner = Corner()
    met = greet_partners()
    r.own_qkv[:, 0:512] = r.own_query[...]
    r.own_qkv[:, 640:1152] = r.own_key[...]
    r.own_qkv[:, 1152:1664] = r.own_value[...]
    r.own_small[...] = jnp.zeros_like(r.own_small)
    vectors = [r.own0, r.own1, r.own2, r.own3, r.own4, r.own5, r.own6, r.own7, r.own8]
    for i, vector in enumerate(vectors):
        r.own_small[i : i + 1, 0 : vector.shape[0]] = wide(vector[...]).reshape(1, vector.shape[0])
    r.own_qkv[:, 512:640] = low(r.own_small[...])
    met()

    def column_part(ref, first, last):
        return ref.at[(slice(None),) * (len(ref.shape) - 1) + (slice(first, last),)]

    def row_part(ref, first, last):
        return ref.at[(slice(None),) * (len(ref.shape) - 2) + (slice(first, last),)]

    pieces = [(column_part, r.own_qkv, r.wqkv, *ends) for ends in ((0, 640), (640, 1152), (1152, 1664))]
    pieces += [(column_part, r.own_output, r.wo, 0, 512)]
    pieces += [(column_part, r.own_inner, r.wi, *ends) for ends in ((0, 1024), (1024, 2048))]
    pieces += [(row_part, r.own_outer, r.wu, *ends) for ends in ((0, 32), (32, 64))]
    gathers = [
        (GatherPlaneFirst if i == U1 else Gather)(corner, cut(own, *ends), cut(whole, *ends), r.gather_send.at[i], r.gather_recv.at[i])
        for i, (cut, own, whole, *ends) in enumerate(pieces)
    ]

    got0 = (r.got0_core, r.got0_b, r.got0_a, r.got0_z)
    got1 = (r.got1_core, r.got1_b, r.got1_a, r.got1_z)
    got2 = (r.got2_core, r.got2_b, r.got2_a, r.got2_z)
    far = (r.far_core, r.far_b, r.far_a, r.far_z)
    pieces = [(column_part, r.gu, r.out_outer, got0, 0, 256), (column_part, r.gu, r.out_outer, far, 256, 512)]
    pieces += [(column_part, r.gi, r.out_inner, got1, *ends) for ends in ((0, 1024), (1024, 2048))]
    pieces += [(column_part, r.go, r.out_output, got2, 0, 512)]
    pieces += [(column_part, r.gqkv, r.out_qkv, spare, *ends) for ends in ((0, 768), (768, 1152), (1152, 1664))]
    kinds = [Scatter, ScatterPlaneLast, *[Scatter] * 5, ScatterDirect]
    scatters = [
        kinds[i](
            corner, cut(whole, *ends), cut(out, *ends), *(got if i < 2 else [cut(ref, *ends) for ref in got]),
            r.scatter_send.at[i], r.scatter_recv.at[i],
        )
        for i, (cut, whole, out, got, *ends) in enumerate(pieces)
    ]
    pieces = gathers + scatters

    def out_away():
        local[2].start()

    def grad_away(side):
        for copy in local[3 + 2 * side : 5 + 2 * side]:
            copy.start()

    def cot_here():
        for piece in gathers:
            piece.finish()
        local[1].wait()

    steps = steps_of(r) | {
        X_HERE: local[0].wait,
        COT_HERE: cot_here,
        OUT_AWAY: out_away,
        GRAD_AWAY0: partial(grad_away, 0),
        GRAD_AWAY1: partial(grad_away, 1),
    }
    def go_all(items):
        for item in items:
            go(item)

    def go(item):
        if isinstance(item, tuple):
            pieces[item[0]].phase(item[1])
        elif isinstance(item, list):
            over_pairs(steps[item[0]], lambda n: go_all(item[1 + n]))
        elif item < X_HERE:
            take(steps[item])
        else:
            steps[item]()

    go_all(PLAN)
    for piece in scatters:
        piece.finish()
    for copy in local[2:]:
        copy.wait()


def received(shard):
    return [(lead + tuple(shard[0]), shard[1]) for lead in ((2, 4, 2), (2, 4), (4,), (3,))]


def direct(inputs, lengths, cotangent, weights, vectors, inner_bias):
    tokens = (TOKENS, WIDTH)
    given = dict(x_far=inputs, cot_far=cotangent, lengths=lengths)
    given |= dict(own_query=weights[0], own_key=weights[1], own_value=weights[2])
    given |= dict(own_output=weights[3], own_inner=weights[4], own_outer=weights[5])
    given |= {"own%d" % i: vector for i, vector in enumerate([*vectors, inner_bias])}
    outputs = dict(
        out_far=(tokens, BF),
        grad_far=(tokens, F32),
        out_qkv=(SHARDS["wqkv"], F32),
        out_output=(SHARDS["wo"], F32),
        out_inner=(SHARDS["wi"], F32),
        out_outer=(SHARDS["wu"], F32),
    )
    whole = {name: (LEAD + shard, BF) for name, shard in SHARDS.items()}
    got0, got1, got2 = [received((shard, BF)) for shard in ((64, 256), (16, 2048), (16, 512))]
    scratch = local_scratch() | whole
    scratch |= dict(
        x=(tokens, BF),
        out=(tokens, BF),
        grad=(tokens, F32),
        gu=whole["wu"],
        go=whole["wo"],
        own_qkv=(SHARDS["wqkv"], BF),
        own_small=((16, LANES), F32),
        vec=((8, WIDTH), F32),
        ib=((1, 2048), F32),
        gvec=((8, WIDTH), F32),
        gib=((1, 2048), F32),
        far_core=got0[0],
        far_b=((2, 64, 256), BF),
        far_a=((64, 256), BF),
        far_z=((3, 2, 2, 64, 256), BF),
        got0_core=got0[0], got0_b=got0[1], got0_a=got0[2], got0_z=got0[3],
        got1_core=got1[0], got1_b=got1[1], got1_a=got1[2], got1_z=got1[3],
        got2_core=got2[0], got2_b=got2[1], got2_a=got2[2], got2_z=got2[3],
    )
    sems = dict(gather_send=(8, 10), gather_recv=(8, 10), scatter_send=(8, 7), scatter_recv=(8, 7), local=(7,))
    spaces = dict(lengths=pltpu.SMEM, x_far=pl.ANY, cot_far=pl.ANY, out_far=pl.ANY, grad_far=pl.ANY)
    made = call(
        direct_kernel, given, spaces, outputs, scratch, sems, collective_id=0, has_side_effects=True
    )
    return hand_over(made)


def hand_over(made):
    count = 4
    rows = TOKENS // count

    def body(out, grad, qkv, output, inner, outer, *refs):
        to_out, to_grad, to_q, to_k, to_v, to_output, to_inner, to_outer = refs[:8]
        vectors, (held_out, held_grad, held_qkv, sem) = refs[8:17], refs[17:]
        copies = []

        def copy(source, target):
            copies.append(pltpu.make_async_copy(source, target, sem.at[len(copies)]))
            copies[-1].start()
            return copies[-1]

        small = copy(qkv, held_qkv)
        parts = []
        for i in range(count):
            part = pl.ds(rows * i, rows)
            for source, held, target in ((grad, held_grad, to_grad), (out, held_out, to_out)):
                parts.append((copy(source.at[part], held.at[part]), held.at[part], target.at[part]))
        to_output[...] = output[...]
        to_inner[...] = inner[...]
        to_outer[...] = outer[...]
        small.wait()
        for i, target in enumerate((to_q, to_k, to_v)):
            for first, last in PAIRS:
                start = 3 * first + (last - first) * i
                target[:, first:last] = held_qkv[:, start : start + last - first]
        for i, target in enumerate(vectors):
            target[...] = held_qkv[i, 1536 : 1536 + target.shape[0]]
        back = []
        for into, held, target in parts:
            into.wait()
            back.append(copy(held, target))
        for each in back:
            each.wait()

    given = [made.out_far, made.grad_far, made.out_qkv, made.out_output, made.out_inner, made.out_outer]
    square = jax.ShapeDtypeStruct((16, 512), F32)
    shapes = [jax.ShapeDtypeStruct(part.shape, part.dtype) for part in given]
    vectors = [jax.ShapeDtypeStruct((16,), F32)] * 8 + [jax.ShapeDtypeStruct((64,), F32)]
    far, near = pl.BlockSpec(memory_space=pl.ANY), pl.BlockSpec(memory_space=pltpu.VMEM)
    out, grad, q, k, v, output, inner, outer, *vectors = pl.pallas_call(
        body,
        out_shape=[*shapes[:2], square, square, square, *shapes[3:], *vectors],
        in_specs=[far, far, far, near, near, near],
        out_specs=[far, far, *[near] * 15],
        scratch_shapes=[
            pltpu.VMEM((TOKENS, WIDTH), BF),
            pltpu.VMEM((TOKENS, WIDTH), F32),
            pltpu.VMEM(SHARDS["wqkv"], F32),
            pltpu.SemaphoreType.DMA((1 + 4 * count,)),
        ],
    )(*given)
    return out, grad, [q, k, v, output, inner, outer], vectors[:8], vectors[8]


def alone_kernel(r):
    r.gi, r.gqkv = halves_of(r.turn)
    r.cot, r.dv, r.dk = r.attended, r.attended, r.hidden
    here = pltpu.make_async_copy(r.cot_far, r.cot, r.local.at[0])
    here.start()
    here.wait()
    run_local(r)
    away = [
        pltpu.make_async_copy(source, target, r.local.at[1 + i])
        for i, (source, target) in enumerate(((r.gi, r.gi_far), (r.gqkv, r.gqkv_far)))
    ]
    for copy in away:
        copy.start()
    for copy in away:
        copy.wait()


def through_collectives(inputs, lengths, cotangent, weights, vectors, inner_bias):
    weights, vectors, inner_bias = jax.tree.map(
        lambda own: lax.all_gather(own, AXES, axis=0, tiled=True), (weights, vectors, inner_bias)
    )
    empty = jnp.zeros((WIDTH, LANES), BF)
    weights = [jnp.concatenate([weights[0], empty, *weights[1:3]], axis=1), *weights[3:]]
    whole = {name: weight.reshape(LEAD + SHARDS[name]) for name, weight in zip(SHARDS, weights)}
    given = dict(x=inputs, cot_far=cotangent, lengths=lengths, **whole)
    given |= dict(vec=jnp.stack(vectors).astype(F32), ib=inner_bias.astype(F32)[None])
    tokens = (TOKENS, WIDTH)
    outputs = dict(out=(tokens, BF), grad=(tokens, F32), gvec=((8, WIDTH), F32), gib=((1, 2048), F32))
    outputs |= dict(gqkv_far=(LEAD + SHARDS["wqkv"], BF), gi_far=(LEAD + SHARDS["wi"], BF))
    outputs |= dict(go=(LEAD + SHARDS["wo"], BF), gu=(LEAD + SHARDS["wu"], BF))
    spaces = dict(lengths=pltpu.SMEM, cot_far=pl.ANY, gqkv_far=pl.ANY, gi_far=pl.ANY)
    scratch = local_scratch() | dict(dq=(tokens, BF))
    made = call(alone_kernel, given, spaces, outputs, scratch, dict(local=(3,)))
    qkv, output, inner, outer = [
        part.reshape(-1, part.shape[-1]).astype(F32) for part in (made.gqkv_far, made.go, made.gi_far, made.gu)
    ]
    grads = []
    for i in range(3):
        starts = [(3 * first + (last - first) * i, last - first) for first, last in PAIRS]
        grads.append(jnp.concatenate([qkv[:, start : start + count] for start, count in starts], axis=1))
    grads += [output, inner, outer]
    grads, vectors, inner_bias = jax.tree.map(
        lambda part: lax.psum_scatter(part, AXES, scatter_dimension=0, tiled=True),
        (grads, [made.gvec[i] for i in range(8)], made.gib[0]),
    )
    return made.out, made.grad, grads, vectors, inner_bias


def solution(mesh):
    on_chips = (mesh.shape["dp"], mesh.shape["fsdp"]) == (4, 8)
    way = direct if on_chips else through_collectives

    def shards(
        inputs, seq_lengths, query_weight, key_weight, value_weight, output_weight, query_bias, value_bias,
        output_bias, first_gain, first_shift, inner_weight, inner_bias, outer_weight, outer_bias, final_gain,
        final_shift, cotangent,
    ):
        weights = [query_weight, key_weight, value_weight, output_weight, inner_weight, outer_weight]
        vectors = [query_bias, value_bias, output_bias, first_gain, first_shift]
        vectors += [outer_bias, final_gain, final_shift]
        out, grad, grads, vectors, inner_total = way(
            inputs, seq_lengths, cotangent, weights, vectors, inner_bias
        )
        return (out, grad, *grads[:4], *vectors[:5], grads[4], inner_total, grads[5], *vectors[5:])

    flat, rows = P(AXES), P(AXES, None)
    weights = (*[rows] * 4, *[flat] * 5, rows, flat, rows, *[flat] * 3)
    return jax.shard_map(
        shards,
        mesh=mesh,
        in_specs=(rows, rows, *weights, rows),
        out_specs=(rows, rows, *weights),
        check_vma=False,
    )
```

profile of v0, /device:TPU:0, one launch (start us, length us, event | category | flops | bytes accessed | tf_op | source)
XLA Modules:
  0.0 98.4 jit_solution(803291525108706954)
XLA Ops:
  0.7 92.9 %shard_map.305 = (bf16[1024,512]{1,0:T(8,128)(2,1)}, f32[1024,512]{1,0:T(8,128)}, f32[16,1664]{1,0:T(8,128)}, f32[16,512]{1,0:T(8,128)}, f32[16,2048]{1,0:T(8,128)}, /*index=5*/f32[64,512]{1,0:T(8,128)}) custom-call(bf16[1024,512]{1,0:T(8,128)(2,1)} %refs_0_.1, bf16[1024,512]{1,0:T(8,128)(2,1)} %refs_1_.1, s32[1,8]{1,0:T(1,128)} %refs_2_.1, ...), custom_call_target="tpu_custom_call" | custom-call | tf_op jit(solution)/shard_map/pallas_call | solution.py:812
  93.5 4.7 %shard_map.306 = (bf16[1024,512]{1,0:T(8,128)(2,1)}, f32[1024,512]{1,0:T(8,128)}, f32[16,512]{1,0:T(8,128)}, f32[16,512]{1,0:T(8,128)}, f32[16,512]{1,0:T(8,128)...) custom-call(bf16[1024,512]{1,0:T(8,128)(2,1)} %get-tuple-element.40., ...), custom_call_target="tpu_custom_call" | custom-call | tf_op jit(solution)/shard_map/pallas_call | solution.py:1082
where the time goes:
time: 98.6 us; the launch traced here: 98.4 us
  Pallas kernels  97.5 us (99%)
    pallas_call x1, Pallas kernels, call(): pl.pallas_call(body, out_shape=[jax.ShapeDtypeStruct(*given) for given in...  92.9 us
    pallas_call x1, Pallas kernels, hand_over(): pl.pallas_call(body, out_shape=[*shapes[:2], square, square, square, *sha...  4.67 us

commit v1 on v0

--- a/solution.py
+++ b/solution.py
@@ -234,10 +234,20 @@
         r.turn[rows, columns] = low(turn)
 
 
+def outer_half(r, rows, side):
+    columns = slice(256 * side, 256 * (side + 1))
+    return nn(r.active[rows], r.wu[:, :, :, :, :, columns].reshape(2048, 256))
+
+
+def first_half_rows(r, i):
+    rows = block_of(i)
+    r.grad[rows, 0:256] = outer_half(r, rows, 0)
+
+
 def final_rows(r, i):
     rows = block_of(i)
     hidden = r.normed[rows] * r.vec[GAIN_ONE : GAIN_ONE + 1] + r.vec[SHIFT_ONE : SHIFT_ONE + 1]
-    outer = nn(r.active[rows], matrix(r.wu)) + r.vec[U_BIAS : U_BIAS + 1]
+    outer = jnp.concatenate([r.grad[rows, 0:256], outer_half(r, rows, 1)], axis=1) + r.vec[U_BIAS : U_BIAS + 1]
     normed, scale = normal(outer + hidden + wide(r.x[rows]))
     gain = r.vec[GAIN_TWO : GAIN_TWO + 1]
     r.out[rows] = low(normed * gain + r.vec[SHIFT_TWO : SHIFT_TWO + 1])
@@ -363,10 +373,10 @@
 
 
 (
-    ZERO, MARK, UNPACK, PROJECT_Q, PROJECT_K, PROJECT_V, ATTEND, ATTENDED, ACTIVE0, ACTIVE1, FINAL, OUTER_GRAD0, OUTER_GRAD1, INNER,
+    ZERO, MARK, UNPACK, PROJECT_Q, PROJECT_K, PROJECT_V, ATTEND, ATTENDED, ACTIVE0, ACTIVE1, FINAL0, FINAL, OUTER_GRAD0, OUTER_GRAD1, INNER,
     INNER_GRAD0, INNER_GRAD1, HIDDEN, OUTPUT_GRAD, PACK_EARLY, BACK, QKV_GRAD0, QKV_GRAD1, QKV_GRAD2, PACK_LATE, INPUT,
-) = range(25)
-LOCAL = [step for step in range(25) if step not in (UNPACK, PACK_EARLY, PACK_LATE)]
+) = range(26)
+LOCAL = [step for step in range(26) if step not in (UNPACK, PACK_EARLY, PACK_LATE)]
 
 
 def all_rows(rows, r, *given):
@@ -396,6 +406,7 @@
         UNPACK: partial(unpack_vectors, r),
         ATTEND: partial(attend, r, at),
         ATTENDED: partial(all_rows, attended_rows, r),
+        FINAL0: partial(all_rows, first_half_rows, r),
         FINAL: partial(all_rows, final_rows, r),
         INNER: partial(all_rows, inner_rows, r),
         HIDDEN: partial(rows_by_two, hidden_rows, r),
@@ -865,17 +876,17 @@
 SU0, SU1, SI0, SI1, SO, SA, SB, SC = range(8, 16)
 X_HERE, COT_HERE, OUT_AWAY, GRAD_AWAY0, GRAD_AWAY1 = range(100, 105)
 PLAN = [
-    (K, 0), (U1, 0), (Q, 0), (V, 0), ZERO, MARK, X_HERE, (U1, 1), (O, 0), (I0, 0), (K, 1), (I1, 0), (Q, 1), (U0, 0),
-    (K, 2), (V, 1), (Q, 2), (O, 1), (V, 2), (I0, 1), (Q, 3), (K, 3), (O, 2), (Q, 4), (U1, 2), UNPACK, PROJECT_Q,
-    (K, 4), (V, 3), (I1, 1), PROJECT_K, (I0, 2), (V, 4), PROJECT_V,
-    [ATTEND, [], [(U0, 1)], [(I1, 2), (O, 3)], [(I0, 3)]], (O, 4), (U0, 2), (I0, 4), ATTENDED, ACTIVE0, (I1, 3),
-    (U1, 3), (U0, 3), (I1, 4), ACTIVE1, (U0, 4), (U1, 4), COT_HERE, FINAL, OUT_AWAY, OUTER_GRAD0, OUTER_GRAD1,
-    (SU0, 0), INNER, (SU1, 0), INNER_GRAD0, (SI0, 0), INNER_GRAD1, (SI1, 0), (SU0, 1), HIDDEN, (SI0, 1), OUTPUT_GRAD,
-    (SO, 0), PACK_EARLY, (SU1, 1), (SI1, 1),
-    [BACK, [], [(SO, 1), (SI0, 2)], [QKV_GRAD0, (SA, 0), (SO, 2), (SU0, 2), (SI1, 2)], [QKV_GRAD1, (SB, 0), (SO, 3), (SA, 1), (SI0, 3), (SU0, 3), (SB, 1)]],
-    (SU1, 2), QKV_GRAD2, (SA, 2), PACK_LATE, (SC, 0), (SI1, 3), (SB, 2), (SC, 1), INPUT, GRAD_AWAY0, GRAD_AWAY1,
-    (SO, 4), (SB, 3), (SA, 3), (SU1, 3), (SC, 2), (SB, 4), (SU0, 4), (SC, 3), (SI0, 4), (SC, 4), (SI1, 4), (SA, 4),
-    (SU1, 4),
+    (Q, 0), (U1, 0), (K, 0), (V, 0), ZERO, MARK, X_HERE, (U1, 1), (O, 0), (I1, 0), (Q, 1), (K, 1), (V, 1), (I0, 0),
+    (U0, 0), (Q, 2), (K, 2), (O, 1), (V, 2), (Q, 3), (I1, 1), (Q, 4), (K, 3), UNPACK, (U1, 2), (V, 3), (I0, 1),
+    (K, 4), PROJECT_Q, (O, 2), (U0, 1), (V, 4), PROJECT_K, PROJECT_V,
+    [ATTEND, [], [(I0, 2)], [(O, 3), (I1, 2)], [(U0, 2), (O, 4)]], (I0, 3), ATTENDED, (I1, 3), (I0, 4), ACTIVE0,
+    (I1, 4), (U0, 3), (U1, 3), ACTIVE1, (U0, 4), FINAL0, (U1, 4), COT_HERE, FINAL, OUT_AWAY, OUTER_GRAD0, OUTER_GRAD1,
+    INNER, (SU0, 0), INNER_GRAD0, INNER_GRAD1, (SU1, 0), (SI1, 0), (SU0, 1), HIDDEN, (SI1, 1), OUTPUT_GRAD, (SU1, 1),
+    (SO, 0), PACK_EARLY, (SU0, 2), (SI0, 0),
+    [BACK, [], [(SO, 1), (SI0, 1)], [QKV_GRAD0, (SU0, 3), (SI1, 2), (SA, 0)], [(SO, 2), (SA, 1), QKV_GRAD1, (SI0, 2), (SI1, 3), (SB, 0)]],
+    (SB, 1), QKV_GRAD2, PACK_LATE, (SC, 0), (SU0, 4), (SO, 3), (SA, 2), (SI0, 3), (SC, 1), INPUT, GRAD_AWAY0,
+    GRAD_AWAY1, (SB, 2), (SO, 4), (SU1, 2), (SA, 3), (SB, 3), (SC, 2), (SC, 3), (SU1, 3), (SU1, 4), (SI1, 4),
+    (SI0, 4), (SB, 4), (SA, 4), (SC, 4),
 ]
 
 
@@ -901,30 +912,39 @@
             + [(r.grad.at[BLOCK * i : BLOCK * (i + 1)], r.grad_far.at[BLOCK * i : BLOCK * (i + 1)]) for i in range(4)]
         )
     ]
-    local[0].start()
-    local[1].start()
+    own = [
+        pltpu.make_async_copy(source, target, r.local.at[7 + i])
+        for i, (source, target) in enumerate(
+            (
+                (r.query_far, r.own_qkv.at[:, 0:512]),
+                (r.key_far, r.own_qkv.at[:, 640:1152]),
+                (r.value_far, r.own_qkv.at[:, 1152:1664]),
+                (r.output_far, r.own_output),
+                (r.inner_far, r.own_inner),
+                (r.outer_far, r.own_outer),
+            )
+        )
+    ]
     corner = Corner()
     met = greet_partners()
-    r.own_qkv[:, 0:512] = r.own_query[...]
-    r.own_qkv[:, 640:1152] = r.own_key[...]
-    r.own_qkv[:, 1152:1664] = r.own_value[...]
+    for copy in (*own, *local[:2]):
+        copy.start()
     r.own_small[...] = jnp.zeros_like(r.own_small)
     vectors = [r.own0, r.own1, r.own2, r.own3, r.own4, r.own5, r.own6, r.own7, r.own8]
     for i, vector in enumerate(vectors):
         r.own_small[i : i + 1, 0 : vector.shape[0]] = wide(vector[...]).reshape(1, vector.shape[0])
     r.own_qkv[:, 512:640] = low(r.own_small[...])
+    for copy in own:
+        copy.wait()
     met()
 
     def column_part(ref, first, last):
         return ref.at[(slice(None),) * (len(ref.shape) - 1) + (slice(first, last),)]
-
-    def row_part(ref, first, last):
-        return ref.at[(slice(None),) * (len(ref.shape) - 2) + (slice(first, last),)]
 
     pieces = [(column_part, r.own_qkv, r.wqkv, *ends) for ends in ((0, 640), (640, 1152), (1152, 1664))]
     pieces += [(column_part, r.own_output, r.wo, 0, 512)]
     pieces += [(column_part, r.own_inner, r.wi, *ends) for ends in ((0, 1024), (1024, 2048))]
-    pieces += [(row_part, r.own_outer, r.wu, *ends) for ends in ((0, 32), (32, 64))]
+    pieces += [(column_part, r.own_outer, r.wu, *ends) for ends in ((0, 256), (256, 512))]
     gathers = [
         (GatherPlaneFirst if i == U1 else Gather)(corner, cut(own, *ends), cut(whole, *ends), r.gather_send.at[i], r.gather_recv.at[i])
         for i, (cut, own, whole, *ends) in enumerate(pieces)
@@ -995,8 +1015,8 @@
 def direct(inputs, lengths, cotangent, weights, vectors, inner_bias):
     tokens = (TOKENS, WIDTH)
     given = dict(x_far=inputs, cot_far=cotangent, lengths=lengths)
-    given |= dict(own_query=weights[0], own_key=weights[1], own_value=weights[2])
-    given |= dict(own_output=weights[3], own_inner=weights[4], own_outer=weights[5])
+    given |= dict(query_far=weights[0], key_far=weights[1], value_far=weights[2])
+    given |= dict(output_far=weights[3], inner_far=weights[4], outer_far=weights[5])
     given |= {"own%d" % i: vector for i, vector in enumerate([*vectors, inner_bias])}
     outputs = dict(
         out_far=(tokens, BF),
@@ -1016,6 +1036,9 @@
         gu=whole["wu"],
         go=whole["wo"],
         own_qkv=(SHARDS["wqkv"], BF),
+        own_output=(SHARDS["wo"], BF),
+        own_inner=(SHARDS["wi"], BF),
+        own_outer=(SHARDS["wu"], BF),
         own_small=((16, LANES), F32),
         vec=((8, WIDTH), F32),
         ib=((1, 2048), F32),
@@ -1029,8 +1052,8 @@
         got1_core=got1[0], got1_b=got1[1], got1_a=got1[2], got1_z=got1[3],
         got2_core=got2[0], got2_b=got2[1], got2_a=got2[2], got2_z=got2[3],
     )
-    sems = dict(gather_send=(8, 10), gather_recv=(8, 10), scatter_send=(8, 7), scatter_recv=(8, 7), local=(7,))
-    spaces = dict(lengths=pltpu.SMEM, x_far=pl.ANY, cot_far=pl.ANY, out_far=pl.ANY, grad_far=pl.ANY)
+    sems = dict(gather_send=(8, 10), gather_recv=(8, 10), scatter_send=(8, 7), scatter_recv=(8, 7), local=(13,))
+    spaces = {name: pl.ANY for name in (*given, *outputs) if name.endswith("_far")} | dict(lengths=pltpu.SMEM)
     made = call(
         direct_kernel, given, spaces, outputs, scratch, sems, collective_id=0, has_side_effects=True
     )
@@ -1052,14 +1075,12 @@
             return copies[-1]
 
         small = copy(qkv, held_qkv)
+        near_ones = [copy(output, to_output), copy(inner, to_inner), copy(outer, to_outer)]
         parts = []
         for i in range(count):
             part = pl.ds(rows * i, rows)
             for source, held, target in ((grad, held_grad, to_grad), (out, held_out, to_out)):
                 parts.append((copy(source.at[part], held.at[part]), held.at[part], target.at[part]))
-        to_output[...] = output[...]
-        to_inner[...] = inner[...]
-        to_outer[...] = outer[...]
         small.wait()
         for i, target in enumerate((to_q, to_k, to_v)):
             for first, last in PAIRS:
@@ -1067,7 +1088,7 @@
                 target[:, first:last] = held_qkv[:, start : start + last - first]
         for i, target in enumerate(vectors):
             target[...] = held_qkv[i, 1536 : 1536 + target.shape[0]]
-        back = []
+        back = near_ones
         for into, held, target in parts:
             into.wait()
             back.append(copy(held, target))
@@ -1082,13 +1103,13 @@
     out, grad, q, k, v, output, inner, outer, *vectors = pl.pallas_call(
         body,
         out_shape=[*shapes[:2], square, square, square, *shapes[3:], *vectors],
-        in_specs=[far, far, far, near, near, near],
+        in_specs=[far] * 6,
         out_specs=[far, far, *[near] * 15],
         scratch_shapes=[
             pltpu.VMEM((TOKENS, WIDTH), BF),
             pltpu.VMEM((TOKENS, WIDTH), F32),
             pltpu.VMEM(SHARDS["wqkv"], F32),
-            pltpu.SemaphoreType.DMA((1 + 4 * count,)),
+            pltpu.SemaphoreType.DMA((4 + 4 * count,)),
         ],
     )(*given)
     return out, grad, [q, k, v, output, inner, outer], vectors[:8], vectors[8]

time: 98.6 us -> 95.9 us (0.973)
  Pallas kernels: 97.5 us -> 94.7 us
    pallas_call x1, Pallas kernels: 92.9 us -> 90.9 us  [call(): pl.pallas_call(body, out_shape=[jax.ShapeDtypeStruct(*given) for given in...]
where the time goes in v1:
time: 95.9 us; the launch traced here: 95.6 us
  Pallas kernels  94.7 us (99%)
    pallas_call x1, Pallas kernels, call(): pl.pallas_call(body, out_shape=[jax.ShapeDtypeStruct(*given) for given in...  90.9 us
    pallas_call x1, Pallas kernels, hand_over(): pl.pallas_call(body, out_shape=[*shapes[:2], square, square, square, *sha...  3.86 us

profile of v1, /device:TPU:0, one launch (start us, length us, event | category | flops | bytes accessed | tf_op | source)
XLA Modules:
  0.0 95.6 jit_solution(16432979202332804796)
XLA Ops:
  0.7 90.9 %shard_map.305 = (bf16[1024,512]{1,0:T(8,128)(2,1)}, f32[1024,512]{1,0:T(8,128)}, f32[16,1664]{1,0:T(8,128)}, f32[16,512]{1,0:T(8,128)}, f32[16,2048]{1,0:T(8,128)}, /*index=5*/f32[64,512]{1,0:T(8,128)}) custom-call(bf16[1024,512]{1,0:T(8,128)(2,1)} %refs_0_.1, bf16[1024,512]{1,0:T(8,128)(2,1)} %refs_1_.1, s32[1,8]{1,0:T(1,128)} %refs_2_.1, ...), custom_call_target="tpu_custom_call" | custom-call | tf_op jit(solution)/shard_map/pallas_call | solution.py:823
  91.6 3.9 %shard_map.306 = (bf16[1024,512]{1,0:T(8,128)(2,1)}, f32[1024,512]{1,0:T(8,128)}, f32[16,512]{1,0:T(8,128)}, f32[16,512]{1,0:T(8,128)}, f32[16,512]{1,0:T(8,128)...) custom-call(bf16[1024,512]{1,0:T(8,128)(2,1)} %get-tuple-element.40., ...), custom_call_target="tpu_custom_call" | custom-call | tf_op jit(solution)/shard_map/pallas_call | solution.py:1103

commit v2 on v1

--- a/solution.py
+++ b/solution.py
@@ -880,13 +880,13 @@
     (U0, 0), (Q, 2), (K, 2), (O, 1), (V, 2), (Q, 3), (I1, 1), (Q, 4), (K, 3), UNPACK, (U1, 2), (V, 3), (I0, 1),
     (K, 4), PROJECT_Q, (O, 2), (U0, 1), (V, 4), PROJECT_K, PROJECT_V,
     [ATTEND, [], [(I0, 2)], [(O, 3), (I1, 2)], [(U0, 2), (O, 4)]], (I0, 3), ATTENDED, (I1, 3), (I0, 4), ACTIVE0,
-    (I1, 4), (U0, 3), (U1, 3), ACTIVE1, (U0, 4), FINAL0, (U1, 4), COT_HERE, FINAL, OUT_AWAY, OUTER_GRAD0, OUTER_GRAD1,
-    INNER, (SU0, 0), INNER_GRAD0, INNER_GRAD1, (SU1, 0), (SI1, 0), (SU0, 1), HIDDEN, (SI1, 1), OUTPUT_GRAD, (SU1, 1),
-    (SO, 0), PACK_EARLY, (SU0, 2), (SI0, 0),
-    [BACK, [], [(SO, 1), (SI0, 1)], [QKV_GRAD0, (SU0, 3), (SI1, 2), (SA, 0)], [(SO, 2), (SA, 1), QKV_GRAD1, (SI0, 2), (SI1, 3), (SB, 0)]],
-    (SB, 1), QKV_GRAD2, PACK_LATE, (SC, 0), (SU0, 4), (SO, 3), (SA, 2), (SI0, 3), (SC, 1), INPUT, GRAD_AWAY0,
-    GRAD_AWAY1, (SB, 2), (SO, 4), (SU1, 2), (SA, 3), (SB, 3), (SC, 2), (SC, 3), (SU1, 3), (SU1, 4), (SI1, 4),
-    (SI0, 4), (SB, 4), (SA, 4), (SC, 4),
+    (I1, 4), (U0, 3), (U1, 3), ACTIVE1, (U0, 4), FINAL0, (U1, 4), COT_HERE, FINAL, OUT_AWAY, OUTER_GRAD0, (SU0, 0),
+    OUTER_GRAD1, INNER, (SU0, 1), INNER_GRAD0, INNER_GRAD1, (SI0, 0), HIDDEN, (SU1, 0), (SI0, 1), OUTPUT_GRAD,
+    PACK_EARLY, (SO, 0), (SU0, 2), (SI1, 0), (SU1, 1),
+    [BACK, [], [(SO, 1), (SI1, 1)], [QKV_GRAD0, (SO, 2), (SI0, 2)], [(SI1, 2), (SA, 0), QKV_GRAD1, (SB, 0), (SO, 3), (SI0, 3), (SA, 1), (SU0, 3), (SB, 1)]],
+    QKV_GRAD2, PACK_LATE, (SA, 2), (SC, 0), (SB, 2), (SO, 4), (SI1, 3), (SC, 1), (SB, 3), (SI0, 4), (SU1, 2), (SA, 3),
+    INPUT, GRAD_AWAY0, GRAD_AWAY1, (SC, 2), (SC, 3), (SB, 4), (SU1, 3), (SI1, 4), (SU1, 4), (SA, 4), (SU0, 4),
+    (SC, 4),
 ]
 
 

time: 95.9 us -> 97 us (1.011)
  Pallas kernels: 94.7 us -> 95.8 us
    pallas_call x1, Pallas kernels: 90.9 us -> 92 us  [call(): pl.pallas_call(body, out_shape=[jax.ShapeDtypeStruct(*given) for given in...]
where the time goes in v2:
time: 97 us; the launch traced here: 96.7 us
  Pallas kernels  95.8 us (99%)
    pallas_call x1, Pallas kernels, call(): pl.pallas_call(body, out_shape=[jax.ShapeDtypeStruct(*given) for given in...  92 us
    pallas_call x1, Pallas kernels, hand_over(): pl.pallas_call(body, out_shape=[*shapes[:2], square, square, square, *sha...  3.86 us

profile of v2, /device:TPU:0, one launch (start us, length us, event | category | flops | bytes accessed | tf_op | source)
XLA Modules:
  0.0 96.7 jit_solution(2092267233304987395)
XLA Ops:
  0.7 92.0 %shard_map.305 = (bf16[1024,512]{1,0:T(8,128)(2,1)}, f32[1024,512]{1,0:T(8,128)}, f32[16,1664]{1,0:T(8,128)}, f32[16,512]{1,0:T(8,128)}, f32[16,2048]{1,0:T(8,128)}, /*index=5*/f32[64,512]{1,0:T(8,128)}) custom-call(bf16[1024,512]{1,0:T(8,128)(2,1)} %refs_0_.1, bf16[1024,512]{1,0:T(8,128)(2,1)} %refs_1_.1, s32[1,8]{1,0:T(1,128)} %refs_2_.1, ...), custom_call_target="tpu_custom_call" | custom-call | tf_op jit(solution)/shard_map/pallas_call | solution.py:823
  92.7 3.9 %shard_map.306 = (bf16[1024,512]{1,0:T(8,128)(2,1)}, f32[1024,512]{1,0:T(8,128)}, f32[16,512]{1,0:T(8,128)}, f32[16,512]{1,0:T(8,128)}, f32[16,512]{1,0:T(8,128)...) custom-call(bf16[1024,512]{1,0:T(8,128)(2,1)} %get-tuple-element.40., ...), custom_call_target="tpu_custom_call" | custom-call | tf_op jit(solution)/shard_map/pallas_call | solution.py:1103
